TPU v7x, 32 devices: a whole 2x2x4 slice. The times are simulated.
32 devices in a mesh: blk: 2 (over core), span: 4 (over y, x), inst: 4 (over z).
Axes of the slice: x: 2, y: 2, z: 4, core: 2. Of those that a mesh axis runs over, the one named last changes fastest.
Arguments:
- source: bfloat16 [4, 16, 81920], P('inst', None, ('blk', 'span')), may hold values from -6 to 6
- jac_interior: bfloat16 [32, 10, 320, 320], P(('blk', 'span', 'inst')), may hold values from -0.25 to 0.25
- interior_rows: int32 [32, 10], P(('blk', 'span', 'inst')), may hold values from 0 to 31
- interior_cols: int32 [32, 10], P(('blk', 'span', 'inst')), may hold values from 0 to 31
- jac_face: bfloat16 [32, 8, 320, 320], P(('blk', 'span', 'inst')), may hold values from -0.25 to 0.25
- face_rows: int32 [32, 8], P(('blk', 'span', 'inst')), may hold values from 0 to 31
- face_cols: int32 [32, 8], P(('blk', 'span', 'inst')), may hold values from 0 to 7, each once within a row
- face_map: int32 [4], replicated, may hold values from 0 to 3, each once
- frequency: float32 [1], replicated, may hold values from 0.04 to 0.1
- surf_mode: int32 [8192, 1], P(('blk', 'span', 'inst')), may hold values from 0 to 1; in each aligned block of 256 rows (0 to 255, 256 to 511, ...) at most 256 rows name the same one
- surf_row: int32 [32, 256], P(('blk', 'span', 'inst')), may hold values from 0 to 10239
- surf_node: int32 [32, 256], P(('blk', 'span', 'inst')), may hold values from 0 to 32767
- mode_shape: float32 [2, 32768], P('blk'), may hold values from -0.4375 to 0.4375
Outputs:
- adjoint: bfloat16 [4, 16, 81920], P('inst', None, ('blk', 'span'))
- modal_grad: float32 [4, 2, 16], P('inst', 'blk')
Inputs may be any that keep to these rules, and one draw needn't show every extreme that they name: `surf_mode`: within the 256 entries of one device no mode is named by more than 256 entries, a bound that some block reaches. `face_cols`: each row names every number below 8 once. `face_map`: each number below 4 once.
All inputs are finite; a program needn't handle non-finite values.
Results may differ from a plain program's by a relative error of at most 0.0051.
Values may be sent and summed in bfloat16 or wider, within the bound.
A program may use at most 64 MiB of HBM per device.

v0:
```python
import functools
import math

import jax
import jax.numpy as jnp
import numpy as np
from jax import lax
from jax.experimental import pallas as pl
from jax.experimental.pallas import tpu as pltpu
from jax.sharding import PartitionSpec as P

ITERS = 6
F32 = jnp.float32
BF16 = jnp.bfloat16


def sweep_kernel(dims, src_ref, jin, jout, icols, fcols, fmap, prev, freq, wt, last_ref, wm_ref,
                 out_ref, mod_ref,
                 srcg, srcb, psi, acc, uown, ugot, faces, lastg, lasts, part, partg,
                 floc, uloc, src_s, src_r, last_s, last_r, loc_sem, face_s, face_r, u_s, u_r, mod_s, mod_r):
    n, nblk, nspan, ni, nf, nb, bs = dims
    blk, span, me = lax.axis_index("blk"), lax.axis_index("span"), lax.axis_index("inst")
    entries = ni + nf

    def inst_peer(d):
        return {"inst": lax.rem(me + d, n)}

    def ring_peer(db, ds):
        return {"blk": lax.rem(blk + db, nblk), "span": lax.rem(span + ds, nspan)}

    others = [(db, ds) for db in range(nblk) for ds in range(nspan) if db or ds]
    barrier = pltpu.get_barrier_semaphore()
    for d in range(1, n):
        pl.semaphore_signal(barrier, inc=1, device_id=inst_peer(d), device_id_type=pl.DeviceIdType.MESH)
    for db, ds in others:
        pl.semaphore_signal(barrier, inc=1, device_id=ring_peer(db, ds), device_id_type=pl.DeviceIdType.MESH)
    pl.semaphore_wait(barrier, n - 1 + len(others))

    def remote(src, dst, send, recv, peer):
        return pltpu.make_async_remote_copy(src_ref=src, dst_ref=dst, send_sem=send, recv_sem=recv,
                                            device_id=peer, device_id_type=pl.DeviceIdType.MESH)

    def last_copy(d):
        return remote(last_ref, lastg.at[n - d - 1], last_s.at[d - 1], last_r.at[n - d - 1], inst_peer(d))

    def src_copy(d):
        return remote(src_ref, srcg.at[n - d - 1], src_s.at[d - 1], src_r.at[n - d - 1], inst_peer(d))

    def u_copy(t, d):
        return remote(uown.at[t], ugot.at[t, n - d - 1], u_s.at[t, d - 1], u_r.at[t, n - d - 1], inst_peer(d))

    def u_wait(t, d):
        remote(uown.at[t], ugot.at[t, d - 1], u_s.at[t, n - d - 1], u_r.at[t, d - 1], inst_peer(d)).wait_recv()
        uloc[d - 1] = ugot[t, d - 1]

    def face_copies(t, par):
        head, tail = psi.at[par, 0, pl.ds(0, 2)], psi.at[par, 0, pl.ds(nb - 2, 2)]
        plan = ((tail, 1, 0), (head, nblk - 1, 0), (tail, 0, 1), (head, 0, nspan - 1))
        return [remote(part_, faces.at[t, k], face_s.at[t, k], face_r.at[t, k], ring_peer(db, ds))
                for k, (part_, db, ds) in enumerate(plan)]

    for d in range(1, n):
        last_copy(d).start()
    for d in range(1, n):
        src_copy(d).start()

    acc[entries] = jnp.zeros_like(acc[entries])

    def relayout(ref, d):
        def body(q, carry):
            pair = ref[:, pl.ds(pl.multiple_of(q * 2 * bs, 128), 2 * bs)]
            srcb[d, 2 * q] = pair[:, :bs]
            srcb[d, 2 * q + 1] = pair[:, bs:]
            return carry
        lax.fori_loop(0, nb // 2, body, 0)

    relayout(src_ref, 0)

    def own_copy(b, carry):
        psi[0, 0, b] = srcb[0, b]
        return carry
    lax.fori_loop(0, nb, own_copy, 0)

    rate = freq[0]

    def weight(di, dj):
        k = lax.rem(me + dj, n) - lax.rem(me + di, n)
        return rate * wt[k + n - 1]

    def products(t, par):
        sends = face_copies(t, par)
        for copy in sends:
            copy.start()
        for e in range(ni):
            x = psi[par, 0, icols[0, e]]
            prod = jnp.dot(x, jin[e], preferred_element_type=F32)
            acc[e] = prod + acc[prev[e]]
        for k, copy in enumerate(sends):
            copy.wait()
            floc[2 * k] = faces[t, k, 0]
            floc[2 * k + 1] = faces[t, k, 1]
        for e in range(nf):
            c = fcols[0, e]
            c = jnp.where(c < 4, fmap[jnp.minimum(c, 3)], c)
            beyond = ((c >= 4) & (c < 6) & (span == 0)) | ((c >= 6) & (span == nspan - 1))
            keep = jnp.where(beyond, 0.0, 1.0)
            x = floc[c]
            prod = jnp.dot(x, jout[e], preferred_element_type=F32) * keep
            acc[ni + e] = prod + acc[prev[ni + e]]

    def send_u(t):
        for e in range(entries):
            uown[t, e] = acc[e].astype(BF16)
        for d in range(1, n):
            u_copy(t, d).start()

    def block(t, par, b, first, final):
        nxt = 1 - par
        if first:
            now = [srcb[d, b].astype(F32) for d in range(1, n)]
        else:
            old = [psi[nxt, d, b].astype(F32) for d in range(n)]
            now = []
            for d in range(1, n):
                at = lasts[d - 1, 0, b]
                got = uloc[d - 1, jnp.minimum(at, entries - 1)].astype(F32)
                val = srcb[d, b].astype(F32) - jnp.where(at < entries, got, 0.0)
                for j in range(n):
                    if j != d:
                        val = val - weight(d, j) * old[j]
                val = val.astype(BF16)
                if not final:
                    psi[par, d, b] = val
                now.append(val.astype(F32))
        if first:
            for d in range(1, n):
                psi[par, d, b] = srcb[d, b]
        val = srcb[0, b].astype(F32) - acc[own_last(b)]
        spec = weight(0, 1) * now[0]
        for d in range(2, n):
            spec = spec + weight(0, d) * now[d - 1]
        val = (val - spec).astype(BF16)
        psi[nxt, 0, b] = val
        return val

    def own_last(b):
        return lasts[n - 1, 0, b]

    def update(t, par, first=False, final=False):
        def body(q, carry):
            lo = block(t, par, 2 * q, first, final)
            hi = block(t, par, 2 * q + 1, first, final)
            if final:
                out_ref[:, pl.ds(pl.multiple_of(q * 2 * bs, 128), 2 * bs)] = jnp.concatenate([lo, hi], axis=1)
                res = []
                for m in range(nblk):
                    tot = carry[m]
                    tot = tot + lo.astype(F32) * wm_ref[2 * q, m:m + 1, :]
                    tot = tot + hi.astype(F32) * wm_ref[2 * q + 1, m:m + 1, :]
                    res.append(tot)
                return tuple(res)
            return carry
        init = tuple(jnp.zeros((src_ref.shape[0], bs), F32) for _ in range(nblk)) if final else 0
        return lax.fori_loop(0, nb // 2, body, init)

    products(0, 0)
    send_u(0)
    for d in range(1, n):
        last_copy(d).wait()
        src_copy(d).wait()
    local = [pltpu.make_async_copy(last_ref, lasts.at[n - 1], loc_sem.at[n - 1])]
    local += [pltpu.make_async_copy(lastg.at[d - 1], lasts.at[d - 1], loc_sem.at[d - 1]) for d in range(1, n)]
    for copy in local:
        copy.start()
    for copy in local:
        copy.wait()
    for d in range(1, n):
        relayout(srcg.at[d - 1], d)
    update(0, 0, first=True)

    def sweep(t, carry):
        par = lax.rem(t, 2)
        products(t, par)
        send_u(t)
        for d in range(1, n):
            u_wait(t - 1, d)
        update(t, par)
        return carry

    lax.fori_loop(1, ITERS - 1, sweep, 0)
    t_end = ITERS - 1
    products(t_end, t_end % 2)
    for d in range(1, n):
        u_wait(t_end - 1, d)
    totals = update(t_end, t_end % 2, final=True)

    for m in range(nblk):
        part[m] = jnp.broadcast_to(jnp.sum(totals[m], axis=1, keepdims=True), part.shape[1:])

    def slot(db, ds):
        return db * nspan + ds - 1

    copies = []
    for db, ds in others:
        mine = slot(db, ds)
        theirs = slot((nblk - db) % nblk, (nspan - ds) % nspan)
        copies.append(remote(part.at[lax.rem(blk + db, nblk)], partg.at[theirs], mod_s.at[mine], mod_r.at[theirs],
                             ring_peer(db, ds)))
    for copy in copies:
        copy.start()
    for copy in copies:
        copy.wait_send()
    total = part[blk]
    for k in range(len(others)):
        copies[k].wait_recv()
    for k in range(len(others)):
        total = total + partg[k]
    mod_ref[...] = total

    def drain(t, carry):
        for d in range(1, n):
            u_copy(t, d).wait_send()
        return carry
    lax.fori_loop(0, ITERS - 1, drain, 0)


def modal_weights(surf_mode, surf_row, surf_node, mode_shape, columns, bs):
    nblk = lax.axis_size("blk")
    lanes = 128
    shapes = lax.all_gather(mode_shape[0], "blk", axis=0, tiled=False)
    nodes = shapes.shape[1]
    e_node, e_row, e_mode = surf_node[0], surf_row[0], surf_mode[:, 0]
    hi = (e_node[:, None] // lanes == jnp.arange(nodes // lanes)[None]).astype(F32)
    lo = (e_node[:, None] % lanes == jnp.arange(lanes)[None]).astype(F32)
    hit = (e_mode[:, None] == jnp.arange(nblk)[None]).astype(F32)
    rows = jnp.einsum("eh,mhl->eml", hi, shapes.reshape(nblk, -1, lanes), precision=lax.Precision.HIGHEST)
    val = jnp.sum(rows * lo[:, None, :], axis=2) * hit
    blocks = (e_row[:, None] // bs == jnp.arange(columns // bs)[None]).astype(F32)
    lane = (e_row[:, None] % bs == jnp.arange(bs)[None]).astype(F32)
    left = (blocks[:, :, None] * jnp.pad(val, ((0, 0), (0, 8 - nblk)))[:, None, :]).reshape(e_row.shape[0], -1)
    return jnp.dot(left.T, lane, precision=lax.Precision.HIGHEST).reshape(columns // bs, 8, bs)


def on_device(source, jac_interior, interior_rows, interior_cols, jac_face, face_rows, face_cols, face_map,
              frequency, surf_mode, surf_row, surf_node, mode_shape):
    r, columns = source.shape[1:]
    ni, bs = jac_interior.shape[1:3]
    nf = jac_face.shape[1]
    nb = columns // bs
    entries = ni + nf
    n, nblk, nspan = lax.axis_size("inst"), lax.axis_size("blk"), lax.axis_size("span")
    ks = np.arange(-(n - 1), n)
    wt = np.array([0.0 if k == 0 else 0.5 * (-1.0) ** int(k) / math.sin(math.pi * k / n) for k in ks], np.float32)
    rows = jnp.concatenate([interior_rows[0], face_rows[0]])
    order = jnp.arange(entries)
    same = (rows[:, None] == rows[None, :]) & (order[None, :] < order[:, None])
    prev = jnp.max(jnp.where(same, order[None, :], -1), axis=1)
    prev = jnp.where(prev < 0, entries, prev).astype(jnp.int32)
    named = rows[None, :] == jnp.arange(128)[:, None]
    last = jnp.max(jnp.where(named, order[None, :], -1), axis=1)
    last = jnp.where(last < 0, entries, last).astype(jnp.int32)
    last = jnp.broadcast_to(last[None], (8, 128))
    wm = modal_weights(surf_mode, surf_row, surf_node, mode_shape, columns, bs)
    vmem = pl.BlockSpec(memory_space=pltpu.VMEM)
    smem = pl.BlockSpec(memory_space=pltpu.SMEM)
    dma = pltpu.SemaphoreType.DMA
    peers = nblk * nspan - 1
    adj, mod = pl.pallas_call(
        functools.partial(sweep_kernel, (n, nblk, nspan, ni, nf, nb, bs)),
        out_shape=(jax.ShapeDtypeStruct((r, columns), BF16), jax.ShapeDtypeStruct((r, 128), F32)),
        in_specs=[vmem, vmem, vmem, smem, smem, smem, smem, smem, smem, vmem, vmem],
        out_specs=(vmem, vmem),
        scratch_shapes=[
            pltpu.VMEM((n - 1, r, columns), BF16),
            pltpu.VMEM((n, nb, r, bs), BF16),
            pltpu.VMEM((2, n, nb, r, bs), BF16),
            pltpu.VMEM((entries + 1, r, bs), F32),
            pltpu.VMEM((ITERS - 1, entries, r, bs), BF16),
            pltpu.VMEM((ITERS - 1, n - 1, entries, r, bs), BF16),
            pltpu.VMEM((ITERS, 4, 2, r, bs), BF16),
            pltpu.VMEM((n - 1, 8, 128), jnp.int32),
            pltpu.SMEM((n, 8, 128), jnp.int32),
            pltpu.VMEM((nblk, r, 128), F32),
            pltpu.VMEM((peers, r, 128), F32),
            pltpu.VMEM((nf, r, bs), BF16),
            pltpu.VMEM((n - 1, entries, r, bs), BF16),
            dma((n - 1,)), dma((n - 1,)), dma((n - 1,)), dma((n - 1,)), dma((n,)),
            dma((ITERS, 4)), dma((ITERS, 4)),
            dma((ITERS - 1, n - 1)), dma((ITERS - 1, n - 1)),
            dma((peers,)), dma((peers,)),
        ],
        compiler_params=pltpu.CompilerParams(
            collective_id=0, has_side_effects=True, vmem_limit_bytes=58 * 2**20),
        name="sweeps",
    )(source[0], jac_interior[0], jac_face[0], interior_cols, face_cols, face_map, prev, frequency,
      jnp.asarray(wt), last, wm)
    return adj[None], mod[:, 0][None, None]


def solution(mesh):
    dev = ("blk", "span", "inst")
    return jax.shard_map(
        on_device,
        mesh=mesh,
        in_specs=(
            P("inst", None, ("blk", "span")),
            P(dev, None, None, None),
            P(dev, None),
            P(dev, None),
            P(dev, None, None, None),
            P(dev, None),
            P(dev, None),
            P(),
            P(),
            P(dev, None),
            P(dev, None),
            P(dev, None),
            P("blk", None),
        ),
        out_specs=(P("inst", None, ("blk", "span")), P("inst", "blk", None)),
        check_vma=False,
    )
```

profile of v0, /device:TPU:9, one launch (start us, length us, event | category | flops | bytes accessed | tf_op | source)
XLA Modules:
  0.0 152.5 jit_solution(6821879432126822946)
XLA Ops:
  1.3 0.7 pad_add_fusion
  2.0 0.2 select_reduce_fusion.1
  2.2 0.1 select_reduce_fusion
  2.3 0.5 compare_select_fusion.2.prev
  2.8 0.7 compare_reduce_fusion
  3.5 0.7 and_select_fusion.2
  4.2 0.7 broadcast_divide_fusion
  4.9 0.6 broadcast_in_dim.39.last_ref
  5.5 2.5 %all-gather = f32[2,1,32768]{2,1,0:T(1,128)S(1)} all-gather(f32[1,1,32768]{2,1,0:T(1,128)} %bitcast.35), channel_id=1, replica_groups=mesh['blk'=2,'span'=4,'inst'=4] {'blk'}, dimensions={0}, use_global_device_ids=true | all-gather | bytes 393216 | tf_op jit(solution)/shard_map/all_gather | solution.py:230
  8.0 0.1 copy.18
  8.2 0.4 multiply_reduce_fusion
  8.6 0.7 compare_select_fusion
  9.3 1.1 fusion.1.wm_ref
  10.4 139.0 %sweeps.1 = (bf16[16,10240]{1,0:T(8,128)(2,1)}, f32[16,128]{1,0:T(8,128)}) custom-call(bf16[16,10240]{1,0:T(8,128)(2,1)} %bitcast.33, bf16[10,320,320]{2,1,0:T(8,128)(2,1)} %bitcast.29, bf16[8,320,320]{2,1,0:T(8,128)(2,1)} %bitcast.30, s32[1,10]{1,0:T(1,128)} %icols.1, s32[1,8]{1,0:T(1,128)} %fcols.1, s32[4]{0:T(128)} %fmap.1, s32[18]{0:T(128)} %compare_select_fusion.2.prev, ...), custom_call_target="tpu_custom_call" | custom-call | tf_op jit(solution)/shard_map/sweeps/pallas_call | solution.py:268
  149.5 1.3 slice_reduce_fusion
  150.8 1.7 %copy.21 = bf16[1,16,10240]{2,1,0:T(8,128)(2,1)} copy(bf16[1,16,10240]{2,1,0:T(8,128)(2,1)} %bitcast.34) | data formatting | bytes 655360
  (5 shorter events, 0.0 us)
where the time goes:
time: 153 us; the launch traced here: 152 us
  Pallas kernels  139 us (91%)
  other arithmetic  4.33 us (3%)
  local copies, waits for them, and re-layouts  3.77 us (2%)
  blocking collectives  2.52 us (2%)
  matrix products  1.57 us (1%)
    pallas_call x1, Pallas kernels, on_device(): pl.pallas_call(functools.partial(sweep_kernel, (n, nblk, nspan, ni, nf, n...  139 us

commit v1 on v0

--- a/solution.py
+++ b/solution.py
@@ -51,7 +51,10 @@
 
     def u_wait(t, d):
         remote(uown.at[t], ugot.at[t, d - 1], u_s.at[t, n - d - 1], u_r.at[t, d - 1], inst_peer(d)).wait_recv()
-        uloc[d - 1] = ugot[t, d - 1]
+        for q in range(entries // 2):
+            pair = ugot[t, d - 1, q]
+            uloc[d - 1, 2 * q] = pair[:, :bs]
+            uloc[d - 1, 2 * q + 1] = pair[:, bs:]
 
     def face_copies(t, par):
         head, tail = psi.at[par, 0, pl.ds(0, 2)], psi.at[par, 0, pl.ds(nb - 2, 2)]
@@ -109,8 +112,8 @@
             acc[ni + e] = prod + acc[prev[ni + e]]
 
     def send_u(t):
-        for e in range(entries):
-            uown[t, e] = acc[e].astype(BF16)
+        for q in range(entries // 2):
+            uown[t, q] = jnp.concatenate([acc[2 * q], acc[2 * q + 1]], axis=1).astype(BF16)
         for d in range(1, n):
             u_copy(t, d).start()
 
@@ -275,8 +278,8 @@
             pltpu.VMEM((n, nb, r, bs), BF16),
             pltpu.VMEM((2, n, nb, r, bs), BF16),
             pltpu.VMEM((entries + 1, r, bs), F32),
-            pltpu.VMEM((ITERS - 1, entries, r, bs), BF16),
-            pltpu.VMEM((ITERS - 1, n - 1, entries, r, bs), BF16),
+            pltpu.VMEM((ITERS - 1, entries // 2, r, 2 * bs), BF16),
+            pltpu.VMEM((ITERS - 1, n - 1, entries // 2, r, 2 * bs), BF16),
             pltpu.VMEM((ITERS, 4, 2, r, bs), BF16),
             pltpu.VMEM((n - 1, 8, 128), jnp.int32),
             pltpu.SMEM((n, 8, 128), jnp.int32),

time: 153 us -> 138 us (0.902)
  Pallas kernels: 139 us -> 123 us
    pallas_call x1, Pallas kernels: 139 us -> 123 us  [on_device(): pl.pallas_call(functools.partial(sweep_kernel, (n, nblk, nspan, ni, nf, n...]
where the time goes in v1:
time: 138 us; the launch traced here: 137 us
  Pallas kernels  123 us (89%)
  other arithmetic  4.33 us (3%)
  local copies, waits for them, and re-layouts  3.77 us (3%)
  blocking collectives  2.52 us (2%)
  matrix products  1.57 us (1%)
    pallas_call x1, Pallas kernels, on_device(): pl.pallas_call(functools.partial(sweep_kernel, (n, nblk, nspan, ni, nf, n...  123 us

profile of v1, /device:TPU:9, one launch (start us, length us, event | category | flops | bytes accessed | tf_op | source)
XLA Modules:
  0.0 136.9 jit_solution(16106903888368645864)
XLA Ops:
  1.3 0.7 pad_add_fusion
  2.0 0.2 select_reduce_fusion.1
  2.2 0.1 select_reduce_fusion
  2.3 0.5 compare_select_fusion.2.prev
  2.8 0.7 compare_reduce_fusion
  3.5 0.7 and_select_fusion.2
  4.2 0.7 broadcast_divide_fusion
  4.9 0.6 broadcast_in_dim.39.last_ref
  5.5 2.5 %all-gather = f32[2,1,32768]{2,1,0:T(1,128)S(1)} all-gather(f32[1,1,32768]{2,1,0:T(1,128)} %bitcast.35), channel_id=1, replica_groups=mesh['blk'=2,'span'=4,'inst'=4] {'blk'}, dimensions={0}, use_global_device_ids=true | all-gather | bytes 393216 | tf_op jit(solution)/shard_map/all_gather | solution.py:233
  8.0 0.1 copy.18
  8.2 0.4 multiply_reduce_fusion
  8.6 0.7 compare_select_fusion
  9.3 1.1 fusion.1.wm_ref
  10.4 123.4 %sweeps.1 = (bf16[16,10240]{1,0:T(8,128)(2,1)}, f32[16,128]{1,0:T(8,128)}) custom-call(bf16[16,10240]{1,0:T(8,128)(2,1)} %bitcast.33, bf16[10,320,320]{2,1,0:T(8,128)(2,1)} %bitcast.29, bf16[8,320,320]{2,1,0:T(8,128)(2,1)} %bitcast.30, s32[1,10]{1,0:T(1,128)} %icols.1, s32[1,8]{1,0:T(1,128)} %fcols.1, s32[4]{0:T(128)} %fmap.1, s32[18]{0:T(128)} %compare_select_fusion.2.prev, ...), custom_call_target="tpu_custom_call" | custom-call | tf_op jit(solution)/shard_map/sweeps/pallas_call | solution.py:271
  133.9 1.3 slice_reduce_fusion
  135.2 1.7 %copy.21 = bf16[1,16,10240]{2,1,0:T(8,128)(2,1)} copy(bf16[1,16,10240]{2,1,0:T(8,128)(2,1)} %bitcast.34) | data formatting | bytes 655360
  (5 shorter events, 0.0 us)

commit v2 on v1

--- a/solution.py
+++ b/solution.py
@@ -17,7 +17,7 @@
 def sweep_kernel(dims, src_ref, jin, jout, icols, fcols, fmap, prev, freq, wt, last_ref, wm_ref,
                  out_ref, mod_ref,
                  srcg, srcb, psi, acc, uown, ugot, faces, lastg, lasts, part, partg,
-                 floc, uloc, src_s, src_r, last_s, last_r, loc_sem, face_s, face_r, u_s, u_r, mod_s, mod_r):
+                 floc, uloc, src_s, src_r, last_s, last_r, loc_sem, face_s, face_r, uo_s, u_s, u_r, mod_s, mod_r):
     n, nblk, nspan, ni, nf, nb, bs = dims
     blk, span, me = lax.axis_index("blk"), lax.axis_index("span"), lax.axis_index("inst")
     entries = ni + nf
@@ -46,15 +46,58 @@
     def src_copy(d):
         return remote(src_ref, srcg.at[n - d - 1], src_s.at[d - 1], src_r.at[n - d - 1], inst_peer(d))
 
-    def u_copy(t, d):
-        return remote(uown.at[t], ugot.at[t, n - d - 1], u_s.at[t, d - 1], u_r.at[t, n - d - 1], inst_peer(d))
-
-    def u_wait(t, d):
-        remote(uown.at[t], ugot.at[t, d - 1], u_s.at[t, n - d - 1], u_r.at[t, d - 1], inst_peer(d)).wait_recv()
-        for q in range(entries // 2):
-            pair = ugot[t, d - 1, q]
-            uloc[d - 1, 2 * q] = pair[:, :bs]
-            uloc[d - 1, 2 * q + 1] = pair[:, bs:]
+    def u_own(t, right):
+        return remote(uown.at[t], ugot.at[t, n - 2 if right else 0], uo_s.at[t, int(right)],
+                      u_r.at[t, n - 2 if right else 0], inst_peer(1 if right else n - 1))
+
+    def u_on(t, d, right):
+        to = max(d - 2, 0) if right else min(d, n - 2)
+        return remote(ugot.at[t, d - 1], ugot.at[t, to], u_s.at[t, d - 1], u_r.at[t, to],
+                      inst_peer(1 if right else n - 1))
+
+    def u_here(t, d):
+        return remote(uown.at[t], ugot.at[t, d - 1], u_s.at[t, d - 1], u_r.at[t, d - 1], inst_peer(1))
+
+    def u_relay(t, o):
+        @pl.when(me >= o)
+        def _():
+            u_here(t, n - o).wait_recv()
+        if o < n - 1:
+            @pl.when((me >= o) & (me < n - 1))
+            def _():
+                u_on(t, n - o, True).start()
+
+        @pl.when(me + o <= n - 1)
+        def _():
+            u_here(t, o).wait_recv()
+        if o < n - 1:
+            @pl.when((me + o <= n - 1) & (me > 0))
+            def _():
+                u_on(t, o, False).start()
+
+    def u_sent(t):
+        @pl.when(me < n - 1)
+        def _():
+            u_own(t, True).wait_send()
+
+        @pl.when(me > 0)
+        def _():
+            u_own(t, False).wait_send()
+        for o in range(1, n - 1):
+            @pl.when((me >= o) & (me < n - 1))
+            def _(o=o):
+                u_on(t, n - o, True).wait_send()
+
+            @pl.when((me + o <= n - 1) & (me > 0))
+            def _(o=o):
+                u_on(t, o, False).wait_send()
+
+    def u_unpack(t):
+        for d in range(1, n):
+            for q in range(entries // 2):
+                pair = ugot[t, d - 1, q]
+                uloc[d - 1, 2 * q] = pair[:, :bs]
+                uloc[d - 1, 2 * q + 1] = pair[:, bs:]
 
     def face_copies(t, par):
         head, tail = psi.at[par, 0, pl.ds(0, 2)], psi.at[par, 0, pl.ds(nb - 2, 2)]
@@ -114,8 +157,14 @@
     def send_u(t):
         for q in range(entries // 2):
             uown[t, q] = jnp.concatenate([acc[2 * q], acc[2 * q + 1]], axis=1).astype(BF16)
-        for d in range(1, n):
-            u_copy(t, d).start()
+
+        @pl.when(me < n - 1)
+        def _():
+            u_own(t, True).start()
+
+        @pl.when(me > 0)
+        def _():
+            u_own(t, False).start()
 
     def block(t, par, b, first, final):
         nxt = 1 - par
@@ -183,18 +232,22 @@
 
     def sweep(t, carry):
         par = lax.rem(t, 2)
+        u_relay(t - 1, 1)
         products(t, par)
+        for o in range(2, n):
+            u_relay(t - 1, o)
         send_u(t)
-        for d in range(1, n):
-            u_wait(t - 1, d)
+        u_unpack(t - 1)
         update(t, par)
         return carry
 
     lax.fori_loop(1, ITERS - 1, sweep, 0)
     t_end = ITERS - 1
+    u_relay(t_end - 1, 1)
     products(t_end, t_end % 2)
-    for d in range(1, n):
-        u_wait(t_end - 1, d)
+    for o in range(2, n):
+        u_relay(t_end - 1, o)
+    u_unpack(t_end - 1)
     totals = update(t_end, t_end % 2, final=True)
 
     for m in range(nblk):
@@ -221,8 +274,7 @@
     mod_ref[...] = total
 
     def drain(t, carry):
-        for d in range(1, n):
-            u_copy(t, d).wait_send()
+        u_sent(t)
         return carry
     lax.fori_loop(0, ITERS - 1, drain, 0)
 
@@ -289,7 +341,7 @@
             pltpu.VMEM((n - 1, entries, r, bs), BF16),
             dma((n - 1,)), dma((n - 1,)), dma((n - 1,)), dma((n - 1,)), dma((n,)),
             dma((ITERS, 4)), dma((ITERS, 4)),
-            dma((ITERS - 1, n - 1)), dma((ITERS - 1, n - 1)),
+            dma((ITERS - 1, 2)), dma((ITERS - 1, n - 1)), dma((ITERS - 1, n - 1)),
             dma((peers,)), dma((peers,)),
         ],
         compiler_params=pltpu.CompilerParams(

time: 138 us -> 136 us (0.986)
  the two profiles are of different devices: /device:TPU:9 before, /device:TPU:0 now
where the time goes in v2:
time: 136 us
  Pallas kernels  123 us (90%)
  other arithmetic  4.33 us (3%)
  local copies, waits for them, and re-layouts  3.77 us (3%)
  blocking collectives  2.3 us (2%)
  matrix products  1.57 us (1%)
    pallas_call x1, Pallas kernels, on_device(): pl.pallas_call(functools.partial(sweep_kernel, (n, nblk, nspan, ni, nf, n...  123 us

profile of v2, /device:TPU:0, one launch (start us, length us, event | category | flops | bytes accessed | tf_op | source)
XLA Modules:
  0.0 136.1 jit_solution(6850839037458141521)
XLA Ops:
  1.3 0.7 pad_add_fusion
  2.0 0.2 select_reduce_fusion.1
  2.2 0.1 select_reduce_fusion
  2.3 0.5 compare_select_fusion.2.prev
  2.8 0.7 compare_reduce_fusion
  3.5 0.7 and_select_fusion.2
  4.2 0.7 broadcast_divide_fusion
  4.9 0.6 broadcast_in_dim.39.last_ref
  5.5 2.3 %all-gather = f32[2,1,32768]{2,1,0:T(1,128)S(1)} all-gather(f32[1,1,32768]{2,1,0:T(1,128)} %bitcast.35), channel_id=1, replica_groups=mesh['blk'=2,'span'=4,'inst'=4] {'blk'}, dimensions={0}, use_global_device_ids=true | all-gather | bytes 393216 | tf_op jit(solution)/shard_map/all_gather | solution.py:285
  7.8 0.1 copy.18
  8.0 0.4 multiply_reduce_fusion
  8.4 0.7 compare_select_fusion
  9.1 1.1 fusion.1.wm_ref
  10.2 122.9 %sweeps.1 = (bf16[16,10240]{1,0:T(8,128)(2,1)}, f32[16,128]{1,0:T(8,128)}) custom-call(bf16[16,10240]{1,0:T(8,128)(2,1)} %bitcast.33, bf16[10,320,320]{2,1,0:T(8,128)(2,1)} %bitcast.29, bf16[8,320,320]{2,1,0:T(8,128)(2,1)} %bitcast.30, s32[1,10]{1,0:T(1,128)} %icols.1, s32[1,8]{1,0:T(1,128)} %fcols.1, s32[4]{0:T(128)} %fmap.1, s32[18]{0:T(128)} %compare_select_fusion.2.prev, ...), custom_call_target="tpu_custom_call" | custom-call | tf_op jit(solution)/shard_map/sweeps/pallas_call | solution.py:323
  133.1 1.3 slice_reduce_fusion
  134.4 1.7 %copy.21 = bf16[1,16,10240]{2,1,0:T(8,128)(2,1)} copy(bf16[1,16,10240]{2,1,0:T(8,128)(2,1)} %bitcast.34) | data formatting | bytes 655360
  (5 shorter events, 0.0 us)
